TPU v7x, 32 devices: a whole 2x2x4 slice. The times are simulated.
32 devices in a mesh: groups: 2 (over x), blk: 16 (over z, y, core).
Axes of the slice: x: 2, y: 2, z: 4, core: 2. Of those that a mesh axis runs over, the one named last changes fastest.
Arguments:
- embedding: bfloat16 [65536, 256], P(('groups', 'blk')), parts along dimension 0, may hold values from -0.7 to 0.7
- assignment: int32 [65536], P(('groups', 'blk')), parts along dimension 0, may hold values from 0 to 127, as said below
- kernel_rate: float32 [2], P('groups'), parts along dimension 0, may hold values from 0.6 to 1.6
Outputs:
- affinity: float32 [65536, 128], P(('groups', 'blk')), parts along dimension 0
- compact: float32 [256], P('groups'), parts along dimension 0
There are 2 independent parts, one for each index of `groups`. A program takes and returns all parts, laid end to end along the dimension named above; each array names one. Nothing has to cross between parts.
Inputs may be any that keep to these rules, and one draw needn't show every extreme that they name: `assignment`: every cluster has at least one node.
All inputs are finite; a program needn't handle non-finite values.
Results may differ from a plain program's by a relative error of at most 0.0005.
Values may be sent and summed in bfloat16 or wider, within the bound.
A program may use at most 64 MiB of HBM per device.

v0:
```python
import jax
import jax.numpy as jnp
from jax import lax
from jax.sharding import PartitionSpec as P

CLUSTERS = 128


def from_behind(x, axis, by):
    count = lax.axis_size(axis)
    return lax.ppermute(x, axis, [(i, (i + by) % count) for i in range(count)])


def one_hot(labels, width):
    return (labels[:, None] == jnp.arange(width, dtype=jnp.int32)[None, :]).astype(jnp.bfloat16)


def kernel_tile(left_rows, right_rows, decay):
    left_norm = jnp.sum(jnp.square(left_rows.astype(jnp.float32)), axis=1)
    right_norm = jnp.sum(jnp.square(right_rows.astype(jnp.float32)), axis=1)
    inner = lax.dot_general(
        left_rows, right_rows, (((1,), (1,)), ((), ())), preferred_element_type=jnp.float32
    )
    return jnp.exp(-decay * (left_norm[:, None] + right_norm[None, :] - 2.0 * inner)).astype(
        jnp.bfloat16
    )


def credit_back(tile, own_hot):
    return lax.dot_general(
        tile, own_hot, (((0,), (0,)), ((), ())), preferred_element_type=jnp.float32
    )


def local(embedding, assignment, kernel_rate):
    width = CLUSTERS
    block_rows = embedding.shape[0]
    decay = kernel_rate[0]
    own_hot = one_hot(assignment, width)
    total = jnp.dot(
        kernel_tile(embedding, embedding, decay), own_hot, preferred_element_type=jnp.float32
    )
    visitor_rows, visitor_labels = (embedding, assignment)
    owed_terms = []
    for offset in range(2):
        visitor_rows, visitor_labels = from_behind((visitor_rows, visitor_labels), "blk", -1)
        tile = kernel_tile(embedding, visitor_rows, decay)
        total = total + jnp.dot(
            tile, one_hot(visitor_labels, width), preferred_element_type=jnp.float32
        )
        owed_terms.append(credit_back(tile, own_hot))
    near_part = from_behind(owed_terms[0], "blk", 1)
    far_part = from_behind(owed_terms[1], "blk", 2)
    total = total + near_part + far_part
    factor = width / (5.0 * block_rows)
    affinity = total * factor
    hot_float = own_hot.astype(jnp.float32)
    mass, count = lax.psum((jnp.sum(total * hot_float, axis=0), jnp.sum(hot_float, axis=0)), "blk")
    compact = mass * factor / count
    return (affinity, compact)


def solution(mesh):
    in_specs = (P(("groups", "blk"), None), P(("groups", "blk")), P("groups"))
    out_specs = (P(("groups", "blk"), None), P("groups"))
    return jax.shard_map(local, mesh=mesh, in_specs=in_specs, out_specs=out_specs, check_vma=False)
```

profile of v0, /device:TPU:0, one launch (start us, length us, event | category | flops | bytes accessed | tf_op | source)
XLA Modules:
  0.0 109.8 jit_solution(16009327541823374300)
XLA Ops:
  0.6 5.5 %collective-permute-start = (bf16[2048,256]{1,0:T(8,128)(2,1)}, bf16[2048,256]{1,0:T(8,128)(2,1)S(1)}, u32[]{:S(2)}, u32[]{:S(2)}) collective-permute-start(bf16[2048,256]{1,0:T(8,128)(2,1)} %param.3), channel_id=1, source_target_pairs={{0,15},{1,0},{2,1},{3,2},{4,3},{5,4},{6,5},{7,6},{8,7},{9,8},{10,9... | collective-permute-start | bytes 3145736 | tf_op jit(solution)/shard_map/ppermute | solution.py:11
  6.1 0.7 collective-permute-start.1
  7.5 1.6 %multiply_reduce_fusion.2 = f32[2048]{0:T(1024)S(1)} fusion(bf16[2048,256]{1,0:T(8,128)(2,1)} %param.3), kind=kLoop, calls=%fused_computation.9 | loop fusion | flops 1570816 | bytes 1056768 | tf_op jit(solution)/shard_map/reduce_sum | solution.py:19
  9.0 9.7 %collective-permute-done = bf16[2048,256]{1,0:T(8,128)(2,1)S(1)} collective-permute-done((bf16[2048,256]{1,0:T(8,128)(2,1)}, bf16[2048,256]{1,0:T(8,128)(2,1)S(1)}, u32[]{:S(2)}, u32[]{:S(2)}) %collective-permute-start) | collective-permute-done | bytes 1048608 | tf_op jit(solution)/shard_map/ppermute | solution.py:11
  18.8 0.3 multiply_reduce_fusion.1
  19.1 4.6 %collective-permute-start.2 = (bf16[2048,256]{1,0:T(8,128)(2,1)S(1)}, bf16[2048,256]{1,0:T(8,128)(2,1)S(1)}, u32[]{:S(2)}, u32[]{:S(2)}) collective-permute-start(bf16[2048,256]{1,0:T(8,128)(2,1)S(1)} %collective-permute-done), channel_id=1, source_target_pairs={{0,15},{1,0},{2,1},{3,2},{4,3},{5,4},{6,5},{7,6},{8,7},{9,8},{10,9... | collective-permute-start | bytes 3145736 | tf_op jit(solution)/shard_map/ppermute | solution.py:11
  23.7 0.0 copy-start.4
  23.7 5.2 %exponential_convert_fusion.1 = bf16[2048,2048]{1,0:T(8,128)(2,1)S(1)} fusion(bf16[2048,256]{1,0:T(8,128)(2,1)} %param.3, bf16[2048,256]{1,0:T(8,128)(2,1)S(1)} %collective-permute-done, f32[2048]{0:T(1024)S(1)} %multiply_reduce_fusion.1, f32[2048]{0:T(1024)S(1)} %multiply_reduce_fusion.2, f32[]{:T(128)} %bitcast), kind=kOutput, calls=%fused_computation.1 | convolution fusion | flops 2168455168 | bytes 10502148 | tf_op jit(solution)/shard_map/dot_general | solution.py:21
  28.9 0.0 copy-done.4
  28.9 0.0 copy-start.2
  28.9 0.0 copy-start.3
  28.9 3.9 %fusion.6 = f32[2048,128]{1,0:T(8,128)} fusion(bf16[2048,2048]{1,0:T(8,128)(2,1)S(1)} %exponential_convert_fusion.1, s32[2048]{0:T(1024)S(1)} %copy-done.4), kind=kOutput, calls=%fused_computation.19 | convolution fusion | flops 1074003968 | bytes 9445376 | tf_op jit(solution)/shard_map/dot_general | solution.py:30
  32.8 0.0 collective-permute-start.4
  32.8 3.2 %collective-permute-done.2 = bf16[2048,256]{1,0:T(8,128)(2,1)S(1)} collective-permute-done((bf16[2048,256]{1,0:T(8,128)(2,1)S(1)}, bf16[2048,256]{1,0:T(8,128)(2,1)S(1)}, u32[]{:S(2)}, u32[]{:S(2)}) %collective-permute-start.2) | collective-permute-done | bytes 1048608 | tf_op jit(solution)/shard_map/ppermute | solution.py:11
  36.0 0.0 copy-done.2
  36.0 0.3 multiply_reduce_fusion
  36.3 0.0 copy-done.3
  36.3 4.2 %exponential_convert_fusion = bf16[2048,2048]{1,0:T(8,128)(2,1)S(1)} fusion(bf16[2048,256]{1,0:T(8,128)(2,1)S(1)} %copy-done.3, bf16[2048,256]{1,0:T(8,128)(2,1)S(1)} %collective-permute-done.2, f32[2048]{0:T(1024)S(1)} %multiply_reduce_fusion, f32[2048]{0:T(1024)S(1)} %multiply_reduce_fusion.2, f32[]{:T(128)} %bitcast), kind=kOutput, calls=%fused_computation | convolution fusion | flops 2168455168 | bytes 10502148 | tf_op jit(solution)/shard_map/dot_general | solution.py:21
  40.6 0.0 copy-start
  40.6 3.2 %copy-done = bf16[2048,2048]{1,0:T(8,128)(2,1)} copy-done((bf16[2048,2048]{1,0:T(8,128)(2,1)}, bf16[2048,2048]{1,0:T(8,128)(2,1)S(1)}, u32[]{:S(2)}) %copy-start) | copy-done | bytes 8388632
  43.8 3.8 %fusion.5 = f32[2048,128]{1,0:T(8,128)} fusion(bf16[2048,2048]{1,0:T(8,128)(2,1)S(1)} %exponential_convert_fusion, s32[2048]{0:T(1024)S(1)} %copy-done.4), kind=kOutput, calls=%fused_computation.18 | convolution fusion | flops 1074003968 | bytes 9445376 | tf_op jit(solution)/shard_map/dot_general | solution.py:30
  47.6 0.0 collective-permute-start.5
  47.6 6.2 %fusion.2 = f32[2048,128]{1,0:T(8,128)S(1)} fusion(bf16[2048,256]{1,0:T(8,128)(2,1)} %param.3, f32[2048]{0:T(1024)S(1)} %multiply_reduce_fusion.2, f32[]{:T(128)} %bitcast, s32[2048]{0:T(1024)S(1)} %copy-done.4), kind=kOutput, calls=%fused_computation.10 | convolution fusion | flops 3242459136 | bytes 2113540 | tf_op jit(solution)/shard_map/dot_general | solution.py:40
  53.8 0.0 copy-start.1
  53.8 0.0 collective-permute-done.1
  53.8 4.8 %collective-permute-start.3 = (s32[2048]{0:T(1024)S(1)}, s32[2048]{0:T(1024)S(1)}, u32[]{:S(2)}, u32[]{:S(2)}) collective-permute-start(s32[2048]{0:T(1024)S(1)} %collective-permute-done.1), channel_id=1, source_target_pairs={{0,15},{1,0},{2,1},{3,2},{4,3},{5,4},{6,5},{7,6},{8,7},{9,8},{10,9... | collective-permute-start | bytes 24584 | tf_op jit(solution)/shard_map/ppermute | solution.py:11
  58.6 5.8 %convolution_add_fusion.1 = f32[2048,128]{1,0:T(8,128)S(1)} fusion(f32[2048,128]{1,0:T(8,128)S(1)} %fusion.2, bf16[2048,2048]{1,0:T(8,128)(2,1)} %copy-done.2, s32[2048]{0:T(1024)S(1)} %collective-permute-done.1), kind=kOutput, calls=%fused_computation.4 | convolution fusion | flops 1074266112 | bytes 10493952 | tf_op jit(solution)/shard_map/dot_general | solution.py:48
  64.5 0.0 collective-permute-done.3
  64.5 0.0 collective-permute-done.4
  64.5 11.9 %collective-permute-done.5 = f32[2048,128]{1,0:T(8,128)S(1)} collective-permute-done((f32[2048,128]{1,0:T(8,128)}, f32[2048,128]{1,0:T(8,128)S(1)}, u32[]{:S(2)}, u32[]{:S(2)}) %collective-permute-start.5) | collective-permute-done | bytes 1048608 | tf_op jit(solution)/shard_map/ppermute | solution.py:11
  76.3 0.0 copy-done.1
  76.3 3.4 %fusion.3 = (f32[128]{0:T(128)S(1)}, f32[128]{0:T(128)S(1)}, f32[2048,128]{1,0:T(8,128)}) fusion(s32[2048]{0:T(1024)S(1)} %copy-done.4, f32[2048,128]{1,0:T(8,128)S(1)} %collective-permute-done.5, f32[2048,128]{1,0:T(8,128)S(1)} %collective-permute-done.4, f32[2048,128]{1,0:T(8,128)S(1)} %convolution_add_fusion.1, bf16[2048,2048]{1,0:T(8,128)(2,1)S(1)} %copy-done.1, ...), kind=kOutput, calls=%fused_computation.13 | convolution fusion | flops 1076625152 | bytes 12600320 | tf_op jit(solution)/shard_map/dot_general | solution.py:48
  79.8 29.5 %all-reduce = (f32[128]{0:T(128)S(1)}, f32[128]{0:T(128)S(1)}) all-reduce(f32[128]{0:T(128)S(1)} %get-tuple-element.3, f32[128]{0:T(128)S(1)} %get-tuple-element.2), channel_id=1, replica_groups=mesh['groups'=2,'blk'=16] {'blk'}, use_global_device_ids=true, to_apply=%region_6.0 | all-reduce | flops 256 | bytes 2048 | tf_op jit(solution)/shard_map/psum | solution.py:58
  109.2 0.5 multiply_divide_fusion
Async XLA Ops:
  0.6 18.1 %collective-permute-start = (bf16[2048,256]{1,0:T(8,128)(2,1)}, bf16[2048,256]{1,0:T(8,128)(2,1)S(1)}, u32[]{:S(2)}, u32[]{:S(2)}) collective-permute-start(bf16[2048,256]{1,0:T(8,128)(2,1)} %param.3), channel_id=1, source_target_pairs={{0,15},{1,0},{2,1},{3,2},{4,3},{5,4},{6,5},{7,6},{8,7},{9,8},{10,9... | collective-permute-start | bytes 3145736 | tf_op jit(solution)/shard_map/ppermute | solution.py:11
  6.1 47.7 %collective-permute-start.1 = (s32[2048]{0:T(1024)}, s32[2048]{0:T(1024)S(1)}, u32[]{:S(2)}, u32[]{:S(2)}) collective-permute-start(s32[2048]{0:T(1024)} %param.4), channel_id=1, source_target_pairs={{0,15},{1,0},{2,1},{3,2},{4,3},{5,4},{6,5},{7,6},{8,7},{9,8},{10,9... | collective-permute-start | bytes 24584 | tf_op jit(solution)/shard_map/ppermute | solution.py:11
  19.1 16.9 %collective-permute-start.2 = (bf16[2048,256]{1,0:T(8,128)(2,1)S(1)}, bf16[2048,256]{1,0:T(8,128)(2,1)S(1)}, u32[]{:S(2)}, u32[]{:S(2)}) collective-permute-start(bf16[2048,256]{1,0:T(8,128)(2,1)S(1)} %collective-permute-done), channel_id=1, source_target_pairs={{0,15},{1,0},{2,1},{3,2},{4,3},{5,4},{6,5},{7,6},{8,7},{9,8},{10,9... | collective-permute-start | bytes 3145736 | tf_op jit(solution)/shard_map/ppermute | solution.py:11
  23.7 5.2 %copy-start.4 = (s32[2048]{0:T(1024)S(1)}, s32[2048]{0:T(1024)}, u32[]{:S(2)}) copy-start(s32[2048]{0:T(1024)} %param.4) | copy-start | bytes 24580
  28.9 7.1 %copy-start.2 = (bf16[2048,2048]{1,0:T(8,128)(2,1)}, bf16[2048,2048]{1,0:T(8,128)(2,1)S(1)}, u32[]{:S(2)}) copy-start(bf16[2048,2048]{1,0:T(8,128)(2,1)S(1)} %exponential_convert_fusion.1) | copy-start | bytes 25165828
  28.9 7.4 %copy-start.3 = (bf16[2048,256]{1,0:T(8,128)(2,1)S(1)}, bf16[2048,256]{1,0:T(8,128)(2,1)}, u32[]{:S(2)}) copy-start(bf16[2048,256]{1,0:T(8,128)(2,1)} %param.3) | copy-start | bytes 3145732
  32.8 31.7 %collective-permute-start.4 = (f32[2048,128]{1,0:T(8,128)}, f32[2048,128]{1,0:T(8,128)S(1)}, u32[]{:S(2)}, u32[]{:S(2)}) collective-permute-start(f32[2048,128]{1,0:T(8,128)} %fusion.6), channel_id=1, source_target_pairs={{0,1},{1,2},{2,3},{3,4},{4,5},{5,6},{6,7},{7,8},{8,9},{9,10},{10,1... | collective-permute-start | bytes 3145736 | tf_op jit(solution)/shard_map/ppermute | solution.py:11
  40.6 3.2 %copy-start = (bf16[2048,2048]{1,0:T(8,128)(2,1)}, bf16[2048,2048]{1,0:T(8,128)(2,1)S(1)}, u32[]{:S(2)}) copy-start(bf16[2048,2048]{1,0:T(8,128)(2,1)S(1)} %exponential_convert_fusion) | copy-start | bytes 25165828
  47.6 28.7 %collective-permute-start.5 = (f32[2048,128]{1,0:T(8,128)}, f32[2048,128]{1,0:T(8,128)S(1)}, u32[]{:S(2)}, u32[]{:S(2)}) collective-permute-start(f32[2048,128]{1,0:T(8,128)} %fusion.5), channel_id=1, source_target_pairs={{0,2},{1,3},{2,4},{3,5},{4,6},{5,7},{6,8},{7,9},{8,10},{9,11},{10,... | collective-permute-start | bytes 3145736 | tf_op jit(solution)/shard_map/ppermute | solution.py:11
  53.8 22.5 %copy-start.1 = (bf16[2048,2048]{1,0:T(8,128)(2,1)S(1)}, bf16[2048,2048]{1,0:T(8,128)(2,1)}, u32[]{:S(2)}) copy-start(bf16[2048,2048]{1,0:T(8,128)(2,1)} %copy-done) | copy-start | bytes 25165828
  53.8 10.6 %collective-permute-start.3 = (s32[2048]{0:T(1024)S(1)}, s32[2048]{0:T(1024)S(1)}, u32[]{:S(2)}, u32[]{:S(2)}) collective-permute-start(s32[2048]{0:T(1024)S(1)} %collective-permute-done.1), channel_id=1, source_target_pairs={{0,15},{1,0},{2,1},{3,2},{4,3},{5,4},{6,5},{7,6},{8,7},{9,8},{10,9... | collective-permute-start | bytes 24584 | tf_op jit(solution)/shard_map/ppermute | solution.py:11
where the time goes:
time: 110 us
  matrix products  32.6 us (30%)
  blocking collectives  29.5 us (27%)
  waiting for transfers between devices  24.8 us (23%)
  starting transfers between devices  15.5 us (14%)
  local copies, waits for them, and re-layouts  3.22 us (3%)
  other arithmetic  2.78 us (3%)
  between operations  1.41 us (1%)
    psum x1, blocking collectives, local(): lax.psum((jnp.sum(total * hot_float, axis=0), jnp.sum(hot_float, axis=0))...  29.5 us
    ppermute x6, waiting for transfers between devices, from_behind(): return lax.ppermute(x, axis, [(i, (i + by) % count) for i in range(count)])  24.8 us
    ppermute x6, starting transfers between devices, from_behind(): return lax.ppermute(x, axis, [(i, (i + by) % count) for i in range(count)])  15.5 us
    dot_general x2, matrix products, kernel_tile(): lax.dot_general(left_rows, right_rows, (((1,), (1,)), ((), ())), preferre...  9.41 us
    dot_general x2, matrix products, local(): jnp.dot(tile, one_hot(visitor_labels, width), preferred_element_type=jnp....  9.27 us
    dot_general x2, matrix products, credit_back(): lax.dot_general(tile, own_hot, (((0,), (0,)), ((), ())), preferred_elemen...  7.69 us
    dot_general x1, matrix products, local(): jnp.dot(kernel_tile(embedding, embedding, decay), own_hot, preferred_elem...  6.22 us
    unnamed x10, local copies, waits for them, and re-layouts  3.22 us
  transfers between devices with their start and end apart: 6, of which 3 were waited for; matrix products, arithmetic and copies ran while one was open for 29% of the time, Pallas kernels for 0%

commit v1 on v0

v1 whole, which is shorter than its diff:
```python
import functools
import math
import jax
import jax.numpy as jnp
from jax import lax
from jax.experimental import pallas as pl
from jax.experimental.pallas import tpu as pltpu
from jax.sharding import PartitionSpec as P

CLUSTERS = 128
CHUNKS = 4
META = 256
NT = (((1,), (1,)), ((), ()))
NEXT_TO = (-2, -1, 1, 2)

OTHER, NEAR, FAR, LENT = range(4)
SCHEDULE = (
    ("own", 0), ("own", 1), ("own", 2), ("own", 3), ("near", 0),
    (OTHER, 0), (OTHER, 1), (OTHER, 2), ("near", 1),
    (OTHER, 3), (NEAR, 0), ("far", 0), (NEAR, 1), ("near", 2),
    (NEAR, 2), (FAR, 0), ("far", 1), (LENT, 0), ("near", 3),
    (NEAR, 3), (FAR, 1), ("far", 2), (LENT, 1), (FAR, 2), ("far", 3),
    (LENT, 2), (FAR, 3), (LENT, 3),
)


def kernel(n, factor, rate_ref, emb_ref, lab_ref, total_ref, compact_ref,
           held, meta, col, hot, parts,
           block_send, block_recv, other_send, other_recv, meta_send, meta_recv,
           part_send, part_recv):
    rows = emb_ref.shape[0]
    size = rows // CHUNKS
    me = lax.axis_index("blk")
    core = lax.rem(me, 2)
    chip = me // 2
    odd = lax.rem(chip, 2)
    step = 1 - 2 * odd
    other = me + 1 - 2 * core
    across = me + 2 * step
    onward = lax.rem(me + 4 * step + n, n)
    lend_near = lax.rem(chip + core, 2) == 0

    barrier = pltpu.get_barrier_semaphore()

    def greet(o, _):
        pl.semaphore_signal(barrier, inc=1, device_id={"blk": lax.rem(me + o, n)},
                            device_id_type=pl.DeviceIdType.MESH)
        return 0

    lax.fori_loop(1, n, greet, 0)

    rate = rate_ref[0] * math.log2(math.e)
    own_meta = 2
    meta[own_meta, 8:16, :] = lab_ref[...].astype(jnp.float32)
    ones = jnp.ones((8, emb_ref.shape[1]), jnp.bfloat16)
    for c in range(CHUNKS):
        e = emb_ref[c * size:(c + 1) * size, :].astype(jnp.float32)
        sq = e * e
        col[c * size:(c + 1) * size, :] = jnp.sum(sq, axis=1, keepdims=True) * -rate
        high = sq.astype(jnp.bfloat16)
        low = (sq - high.astype(jnp.float32)).astype(jnp.bfloat16)
        line = (lax.dot_general(ones, high, NT, preferred_element_type=jnp.float32)
                + lax.dot_general(ones, low, NT, preferred_element_type=jnp.float32)) * -rate
        for q in range(size // META):
            r = c * (size // META) + q
            meta[own_meta, r:r + 1, :] = line[0:1, q * META:(q + 1) * META]

    pl.semaphore_wait(barrier, n - 1)

    def remote(src, dst, send, recv, peer):
        return pltpu.make_async_remote_copy(
            src_ref=src, dst_ref=dst, send_sem=send, recv_sem=recv,
            device_id={"blk": peer}, device_id_type=pl.DeviceIdType.MESH)

    def piece(c):
        return pl.ds(c * size, size)

    to_near = [remote(emb_ref.at[piece(c)], held.at[NEAR, piece(c)],
                      block_send.at[0, c], block_recv.at[0, c], across) for c in range(CHUNKS)]
    to_far = [remote(held.at[NEAR, piece(c)], held.at[FAR, piece(c)],
                     block_send.at[1, c], block_recv.at[1, c], onward) for c in range(CHUNKS)]
    lend_slot = jnp.where(lend_near, NEAR, FAR)
    to_lent = [remote(held.at[lend_slot, piece(c)], held.at[LENT, piece(c)],
                      block_send.at[2, c], block_recv.at[2, c], other) for c in range(CHUNKS)]
    to_other = remote(emb_ref, held.at[OTHER], other_send, other_recv, other)
    to_meta = [remote(meta.at[own_meta], meta.at[2 - o], meta_send.at[i], meta_recv.at[i],
                      lax.rem(me + o + n, n)) for i, o in enumerate(NEXT_TO)]

    for copy in to_meta:
        copy.start()
    to_other.start()
    for copy in to_near:
        copy.start()

    def hot_line(slot, c):
        first = c * (size // META)
        lab = jnp.concatenate(
            [meta[slot, 8 + first + q:9 + first + q, :] for q in range(size // META)], axis=1)
        line = lax.broadcasted_iota(jnp.int32, (CLUSTERS, size), 0).astype(jnp.float32)
        return line == lab

    for c in range(CHUNKS):
        picked = jnp.where(hot_line(own_meta, c), 1.0, 0.0)
        hot[c * size:(c + 1) * size, :] = jnp.transpose(picked)

    total_ref[...] = jnp.zeros_like(total_ref)
    slots = {
        OTHER: 3 - 2 * core, NEAR: 2 + 2 * step, FAR: 2 - 2 * step, LENT: 1 + 2 * core,
    }

    def work(block, slot, c):
        first = c * (size // META)
        norm = jnp.concatenate(
            [meta[slot, first + q:first + q + 1, :] for q in range(size // META)], axis=1)
        right_hot = hot_line(slot, c).astype(jnp.float32).astype(jnp.bfloat16)
        right = block[piece(c), :]

        def left(i, _):
            r = pl.ds(pl.multiple_of(i * size, size), size)
            inner = lax.dot_general(emb_ref[r, :], right, NT, preferred_element_type=jnp.float32)
            tile = jnp.exp2(inner * (2.0 * rate) + (col[r, :] + norm)).astype(jnp.bfloat16)
            total_ref[r, :] += lax.dot_general(
                tile, right_hot, NT, preferred_element_type=jnp.float32)
            return 0

        lax.fori_loop(0, rows // size, left, 0, unroll=2)

    for what, c in SCHEDULE:
        if what == "own":
            work(emb_ref, own_meta, c)
        elif what == "near":
            to_near[c].wait_recv()
            to_far[c].start()

            @pl.when(lend_near)
            def _():
                to_lent[c].start()
        elif what == "far":
            to_far[c].wait_recv()

            @pl.when(jnp.logical_not(lend_near))
            def _():
                to_lent[c].start()
        else:
            if what == OTHER and c == 0:
                to_other.wait_recv()
                for copy in to_meta:
                    copy.wait_recv()
            if what == LENT:
                to_lent[c].wait_recv()
            work(held.at[what], slots[what], c)

    total = total_ref[...]
    own_hot = hot[...]
    mass = jnp.sum(total * own_hot, axis=0, keepdims=True)
    count = jnp.sum(own_hot, axis=0, keepdims=True)
    parts[me, 0:1, :] = mass
    parts[me, 1:2, :] = count

    def to_part(o):
        return remote(parts.at[me], parts.at[me], part_send.at[o], part_recv.at[o],
                      lax.rem(me + o, n))

    def send_part(o, _):
        to_part(o).start()
        return 0

    lax.fori_loop(1, n, send_part, 0)
    total_ref[...] = total * factor
    for copy in to_meta + [to_other] + to_near + to_far + to_lent:
        copy.wait_send()

    def end_part(o, _):
        source = lax.rem(me - o + n, n)
        remote(parts.at[me], parts.at[source], part_send.at[o], part_recv.at[o],
               lax.rem(me + o, n)).wait()
        return 0

    lax.fori_loop(1, n, end_part, 0)

    masses = jnp.sum(parts[:, 0:1, :], axis=0)
    counts = jnp.sum(parts[:, 1:2, :], axis=0)
    compact_ref[...] = masses * factor / counts


def local(n, embedding, assignment, kernel_rate):
    rows, width = embedding.shape
    factor = CLUSTERS / (5.0 * rows)
    dma = pltpu.SemaphoreType.DMA
    affinity, compact = pl.pallas_call(
        functools.partial(kernel, n, factor),
        out_shape=(jax.ShapeDtypeStruct((rows, CLUSTERS), jnp.float32),
                   jax.ShapeDtypeStruct((1, CLUSTERS), jnp.float32)),
        in_specs=[pl.BlockSpec(memory_space=pltpu.SMEM),
                  pl.BlockSpec(memory_space=pltpu.VMEM),
                  pl.BlockSpec(memory_space=pltpu.VMEM)],
        out_specs=[pl.BlockSpec(memory_space=pltpu.VMEM)] * 2,
        scratch_shapes=[
            pltpu.VMEM((4, rows, width), jnp.bfloat16),
            pltpu.VMEM((5, 16, META), jnp.float32),
            pltpu.VMEM((rows, 1), jnp.float32),
            pltpu.VMEM((rows, CLUSTERS), jnp.float32),
            pltpu.VMEM((n, 8, CLUSTERS), jnp.float32),
            dma((3, CHUNKS)), dma((3, CHUNKS)), dma, dma, dma((4,)), dma((4,)),
            dma((n,)), dma((n,)),
        ],
        compiler_params=pltpu.CompilerParams(
            collective_id=0, has_side_effects=True, vmem_limit_bytes=48 * 2**20),
        name="affinities",
    )(kernel_rate, embedding, assignment.reshape(rows // META, META))
    return affinity, compact.reshape(CLUSTERS)


def solution(mesh):
    n = mesh.shape["blk"]
    in_specs = (P(("groups", "blk"), None), P(("groups", "blk")), P("groups"))
    out_specs = (P(("groups", "blk"), None), P("groups"))
    return jax.shard_map(functools.partial(local, n), mesh=mesh, in_specs=in_specs,
                         out_specs=out_specs, check_vma=False)
```

time: 110 us -> 54.5 us (0.50)
  Pallas kernels: 0 us -> 49.6 us
  matrix products: 32.6 us -> 0 us
  blocking collectives: 29.5 us -> 0 us
  waiting for transfers between devices: 24.8 us -> 0 us
  starting transfers between devices: 15.5 us -> 0 us
  other arithmetic: 2.78 us -> 0 us
    pallas_call x0 -> x1, Pallas kernels: none -> 49.6 us  [local(): pl.pallas_call(functools.partial(kernel, n, factor), out_shape=(jax.Shape...]
    dot_general x7 -> x0, matrix products: 32.6 us -> none  [the longest x2 9.41 us: kernel_tile(): lax.dot_general(left_rows, right_rows, (((1,), (1,)), ((), ())), preferre...]
    psum x1 -> x0, blocking collectives: 29.5 us -> none  [local(): lax.psum((jnp.sum(total * hot_float, axis=0), jnp.sum(hot_float, axis=0))...]
    ppermute x6 -> x0, waiting for transfers between devices: 24.8 us -> none  [from_behind(): return lax.ppermute(x, axis, [(i, (i + by) % count) for i in range(count)])]
    ppermute x6 -> x0, starting transfers between devices: 15.5 us -> none  [from_behind(): return lax.ppermute(x, axis, [(i, (i + by) % count) for i in range(count)])]
    reduce_sum x3 -> x0, other arithmetic: 2.26 us -> none  [the longest x1 1.57 us: kernel_tile(): left_norm = jnp.sum(jnp.square(left_rows.astype(jnp.float32)), axis=1)]
    unnamed x10 -> x4, local copies, waits for them, and re-layouts: 3.22 us -> 2.71 us
  transfers between devices with their start and end apart: 6 -> 0, of which waited for: 3 -> 0; matrix products, arithmetic and copies ran while one was open for 29% -> 0% of each run, Pallas kernels for 0% -> 0%
where the time goes in v1:
time: 54.5 us; the launch traced here: 54.3 us
  Pallas kernels  49.6 us (91%)
  local copies, waits for them, and re-layouts  3.41 us (6%)
  between operations  1.29 us (2%)
    pallas_call x1, Pallas kernels, local(): pl.pallas_call(functools.partial(kernel, n, factor), out_shape=(jax.Shape...  49.6 us
    unnamed x4, local copies, waits for them, and re-layouts  2.71 us

profile of v1, /device:TPU:0, one launch (start us, length us, event | category | flops | bytes accessed | tf_op | source)
XLA Modules:
  0.0 54.3 jit_solution(18216344669911893357)
XLA Ops:
  1.3 0.7 %reshape.10.lab_ref = s32[8,256]{1,0:T(8,128)S(1)} reshape(s32[2048]{0:T(1024)} %param.4) | data formatting | bytes 16384 | tf_op jit(solution)/shard_map/reshape | solution.py:210
  2.0 0.0 copy-start
  2.0 1.2 %copy-done = bf16[2048,256]{1,0:T(8,128)(2,1)S(1)} copy-done((bf16[2048,256]{1,0:T(8,128)(2,1)S(1)}, bf16[2048,256]{1,0:T(8,128)(2,1)}, u32[]{:S(2)}) %copy-start) | copy-done | bytes 1048600
  3.2 49.6 %affinities.1 = (f32[2048,128]{1,0:T(8,128)S(1)}, f32[1,128]{1,0:T(1,128)S(1)}) custom-call(f32[1]{0:T(128)S(6)} %copy.7.rate_ref, bf16[2048,256]{1,0:T(8,128)(2,1)S(1)} %copy-done, s32[8,256]{1,0:T(8,128)S(1)} %reshape.10.lab_ref), custom_call_target="tpu_custom_call" | custom-call | tf_op jit(solution)/shard_map/affinities/pallas_call | solution.py:190
  52.8 1.0 %copy.8 = f32[2048,128]{1,0:T(8,128)} copy(f32[2048,128]{1,0:T(8,128)S(1)} %get-tuple-element.8) | data formatting | bytes 2097152
  53.8 0.5 copy.9
Async XLA Ops:
  2.0 1.2 %copy-start = (bf16[2048,256]{1,0:T(8,128)(2,1)S(1)}, bf16[2048,256]{1,0:T(8,128)(2,1)}, u32[]{:S(2)}) copy-start(bf16[2048,256]{1,0:T(8,128)(2,1)} %emb_ref.1) | copy-start | bytes 3145732

commit v2 on v1

v2 whole, which is shorter than its diff:
```python
import functools
import math
import jax
import jax.numpy as jnp
from jax import lax
from jax.experimental import pallas as pl
from jax.experimental.pallas import tpu as pltpu
from jax.sharding import PartitionSpec as P

CLUSTERS = 128
META = 256
NT = (((1,), (1,)), ((), ()))
NEXT_TO = (-2, -1, 1, 2)

OTHER, NEAR, FAR, LENT, OWN = range(5)
QUARTERS = 4
ORDER = (
    (OWN, 0), (OWN, 1), (OWN, 2), (OWN, 3), (OTHER, 0), (OTHER, 1), (OTHER, 2),
    (NEAR, 0), (FAR, 0), (LENT, 0), (NEAR, 1), (FAR, 1), (LENT, 1), (NEAR, 2),
    (OTHER, 3), (FAR, 2), (LENT, 2), (NEAR, 3), (FAR, 3), (LENT, 3),
)


def lookup(step, values):
    found = jnp.int32(values[0])
    for k, value in enumerate(values):
        if k and value != values[k - 1]:
            found = jnp.where(step >= k, jnp.int32(value), found)
    return found


def kernel(n, factor, rate_ref, emb_ref, lab_ref, total_ref, compact_ref,
           held, meta, line, sums, parts, own_copy,
           block_send, block_recv, other_send, other_recv, meta_send, meta_recv,
           part_send, part_recv):
    rows = emb_ref.shape[0]
    size = rows // QUARTERS
    chunks = rows // META
    me = lax.axis_index("blk")
    core = lax.rem(me, 2)
    chip = me // 2
    odd = lax.rem(chip, 2)
    step_to = 1 - 2 * odd
    other = me + 1 - 2 * core
    across = me + 2 * step_to
    onward = lax.rem(me + 4 * step_to + n, n)
    lend_near = lax.rem(chip + core, 2) == 0

    barrier = pltpu.get_barrier_semaphore()

    def greet(o, _):
        pl.semaphore_signal(barrier, inc=1, device_id={"blk": lax.rem(me + o, n)},
                            device_id_type=pl.DeviceIdType.MESH)
        return 0

    lax.fori_loop(1, n, greet, 0)
    own = pltpu.make_async_copy(emb_ref, held.at[OWN], own_copy)
    own.start()
    meta[2] = lab_ref[...]
    sums[...] = jnp.zeros_like(sums)
    pl.semaphore_wait(barrier, n - 1)

    def remote(src, dst, send, recv, peer):
        return pltpu.make_async_remote_copy(
            src_ref=src, dst_ref=dst, send_sem=send, recv_sem=recv,
            device_id={"blk": peer}, device_id_type=pl.DeviceIdType.MESH)

    def piece(c):
        return pl.ds(pl.multiple_of(c * META, META), META)

    def to_near(c):
        return remote(emb_ref.at[piece(c)], held.at[NEAR, piece(c)],
                      block_send.at[0, c], block_recv.at[0, c], across)

    def to_far(c):
        return remote(held.at[NEAR, piece(c)], held.at[FAR, piece(c)],
                      block_send.at[1, c], block_recv.at[1, c], onward)

    lend_slot = jnp.where(lend_near, NEAR, FAR)

    def to_lent(c):
        return remote(held.at[lend_slot, piece(c)], held.at[LENT, piece(c)],
                      block_send.at[2, c], block_recv.at[2, c], other)

    to_other = remote(emb_ref, held.at[OTHER], other_send, other_recv, other)
    to_meta = [remote(lab_ref, meta.at[2 - o], meta_send.at[i], meta_recv.at[i],
                      lax.rem(me + o + n, n)) for i, o in enumerate(NEXT_TO)]

    to_near(0).start()
    to_other.start()
    for copy in to_meta:
        copy.start()

    def send_near(c, _):
        to_near(c).start()
        return 0

    lax.fori_loop(1, chunks, send_near, 0)
    own.wait()

    rate = rate_ref[0] * math.log2(math.e)
    ones = jnp.ones((8, emb_ref.shape[1]), jnp.bfloat16)

    def own_norm(c, _):
        r = pl.ds(pl.multiple_of(c * size, size), size)
        e = held[OWN, r, :].astype(jnp.float32)
        sq = e * e
        high = sq.astype(jnp.bfloat16)
        low = (sq - high.astype(jnp.float32)).astype(jnp.bfloat16)
        norm = (lax.dot_general(ones, high, NT, preferred_element_type=jnp.float32)
                + lax.dot_general(ones, low, NT, preferred_element_type=jnp.float32))
        line[:, r] = norm[0:1, :] * -rate
        return 0

    lax.fori_loop(0, QUARTERS, own_norm, 0)

    def hot_rows(slot, c):
        first = c * (size // META)
        lab = jnp.concatenate(
            [meta[slot, pl.ds(first + q, 1), :] for q in range(size // META)], axis=1)
        return lax.broadcasted_iota(jnp.int32, (CLUSTERS, size), 0) == lab

    def as_line(x):
        width = x.shape[1]
        folded = x[:, 0:CLUSTERS]
        for q in range(1, width // CLUSTERS):
            folded = folded + x[:, q * CLUSTERS:(q + 1) * CLUSTERS]
        return jnp.sum(jnp.transpose(folded), axis=0, keepdims=True)

    count = sum(as_line(jnp.where(hot_rows(2, c), 1.0, 0.0)) for c in range(QUARTERS))
    parts[me, 1:2, :] = count

    blocks = [block for block, _ in ORDER]
    quarters = [c for _, c in ORDER]

    def work(step, _):
        @pl.when(jnp.logical_and(lax.rem(step, 2) == 0,
                                 jnp.logical_and(step >= 2, step <= 16)))
        def _():
            c = (step - 2) // 2
            to_near(c).wait_recv()
            to_far(c).start()

            @pl.when(lend_near)
            def _():
                to_lent(c).start()

        @pl.when(jnp.logical_or(
            jnp.logical_and(lax.rem(step, 2) == 1,
                            jnp.logical_and(step >= 5, step <= 17)), step == 18))
        def _():
            c = (step - 4) // 2
            to_far(c).wait_recv()

            @pl.when(jnp.logical_not(lend_near))
            def _():
                to_lent(c).start()

        @pl.when(step == 4)
        def _():
            to_other.wait_recv()
            for copy in to_meta:
                copy.wait_recv()

        block = lookup(step, blocks)
        quarter = lookup(step, quarters)

        @pl.when(block == LENT)
        def _():
            to_lent(2 * quarter).wait_recv()
            to_lent(2 * quarter + 1).wait_recv()

        slot = jnp.where(block == OWN, 2, jnp.where(
            block == OTHER, 3 - 2 * core, jnp.where(
                block == NEAR, 2 + 2 * step_to, jnp.where(
                    block == FAR, 2 - 2 * step_to, 1 + 2 * core))))
        right = held[block, pl.ds(pl.multiple_of(quarter * size, size), size), :]
        right_hot = hot_rows(slot, quarter).astype(jnp.float32).astype(jnp.bfloat16)
        wide = right.astype(jnp.float32)
        norm = jnp.sum(wide * wide, axis=1, keepdims=True) * -rate
        inner = lax.dot_general(right, held[OWN], NT, preferred_element_type=jnp.float32)
        tile = jnp.exp2(inner * (2.0 * rate) + (norm + line[...])).astype(jnp.bfloat16)
        sums[...] += jnp.dot(right_hot, tile, preferred_element_type=jnp.float32)
        return 0

    lax.fori_loop(0, len(ORDER), work, 0)

    mass = sum(as_line(jnp.where(hot_rows(2, c), sums[:, c * size:(c + 1) * size], 0.0))
               for c in range(QUARTERS))
    parts[me, 0:1, :] = mass

    def send_part(o, _):
        remote(parts.at[me], parts.at[me], part_send.at[o], part_recv.at[o],
               lax.rem(me + o, n)).start()
        return 0

    lax.fori_loop(1, n, send_part, 0)
    for q in range(rows // CLUSTERS):
        r = slice(q * CLUSTERS, (q + 1) * CLUSTERS)
        total_ref[r, :] = jnp.transpose(sums[:, r]) * factor
    for copy in to_meta + [to_other]:
        copy.wait_send()

    def end_sends(c, _):
        to_near(c).wait_send()
        to_far(c).wait_send()
        to_lent(c).wait_send()
        return 0

    lax.fori_loop(0, chunks, end_sends, 0)

    def end_part(o, _):
        source = lax.rem(me - o + n, n)
        remote(parts.at[me], parts.at[source], part_send.at[o], part_recv.at[o],
               lax.rem(me + o, n)).wait()
        return 0

    lax.fori_loop(1, n, end_part, 0)

    masses = jnp.sum(parts[:, 0:1, :], axis=0)
    counts = jnp.sum(parts[:, 1:2, :], axis=0)
    compact_ref[...] = masses * factor / counts


def local(n, embedding, assignment, kernel_rate):
    rows, width = embedding.shape
    factor = CLUSTERS / (5.0 * rows)
    dma = pltpu.SemaphoreType.DMA
    affinity, compact = pl.pallas_call(
        functools.partial(kernel, n, factor),
        out_shape=(jax.ShapeDtypeStruct((rows, CLUSTERS), jnp.float32),
                   jax.ShapeDtypeStruct((1, CLUSTERS), jnp.float32)),
        in_specs=[pl.BlockSpec(memory_space=pltpu.SMEM),
                  pl.BlockSpec(memory_space=pl.ANY),
                  pl.BlockSpec(memory_space=pltpu.VMEM)],
        out_specs=[pl.BlockSpec(memory_space=pltpu.VMEM)] * 2,
        scratch_shapes=[
            pltpu.VMEM((5, rows, width), jnp.bfloat16),
            pltpu.VMEM((5, rows // META, META), jnp.int32),
            pltpu.VMEM((1, rows), jnp.float32),
            pltpu.VMEM((CLUSTERS, rows), jnp.float32),
            pltpu.VMEM((n, 8, CLUSTERS), jnp.float32),
            dma, dma((3, rows // META)), dma((3, rows // META)), dma, dma, dma((4,)), dma((4,)),
            dma((n,)), dma((n,)),
        ],
        compiler_params=pltpu.CompilerParams(
            collective_id=0, has_side_effects=True, vmem_limit_bytes=48 * 2**20),
        name="affinities",
    )(kernel_rate, embedding, assignment.reshape(rows // META, META))
    return affinity, compact.reshape(CLUSTERS)


def solution(mesh):
    n = mesh.shape["blk"]
    in_specs = (P(("groups", "blk"), None), P(("groups", "blk")), P("groups"))
    out_specs = (P(("groups", "blk"), None), P("groups"))
    return jax.shard_map(functools.partial(local, n), mesh=mesh, in_specs=in_specs,
                         out_specs=out_specs, check_vma=False)
```

time: 54.5 us -> 48.8 us (0.90)
  Pallas kernels: 49.6 us -> 43.9 us
    pallas_call x1, Pallas kernels: 49.6 us -> 43.9 us  [local(): pl.pallas_call(functools.partial(kernel, n, factor), out_shape=(jax.Shape...]
where the time goes in v2:
time: 48.8 us; the launch traced here: 48.6 us
  Pallas kernels  43.9 us (90%)
  local copies, waits for them, and re-layouts  3.41 us (7%)
  between operations  1.29 us (3%)
    pallas_call x1, Pallas kernels, local(): pl.pallas_call(functools.partial(kernel, n, factor), out_shape=(jax.Shape...  43.9 us
    unnamed x4, local copies, waits for them, and re-layouts  2.71 us

profile of v2, /device:TPU:0, one launch (start us, length us, event | category | flops | bytes accessed | tf_op | source)
XLA Modules:
  0.0 48.6 jit_solution(8526085421944578548)
XLA Ops:
  1.3 0.7 %reshape.10.lab_ref = s32[8,256]{1,0:T(8,128)S(1)} reshape(s32[2048]{0:T(1024)} %param.4) | data formatting | bytes 16384 | tf_op jit(solution)/shard_map/reshape | solution.py:249
  2.0 0.0 copy-start
  2.0 1.2 %copy-done = bf16[2048,256]{1,0:T(8,128)(2,1)S(1)} copy-done((bf16[2048,256]{1,0:T(8,128)(2,1)S(1)}, bf16[2048,256]{1,0:T(8,128)(2,1)}, u32[]{:S(2)}) %copy-start) | copy-done | bytes 1048600
  3.2 43.9 %affinities.1 = (f32[2048,128]{1,0:T(8,128)S(1)}, f32[1,128]{1,0:T(1,128)S(1)}) custom-call(f32[1]{0:T(128)S(6)} %copy.7.rate_ref, bf16[2048,256]{1,0:T(8,128)(2,1)S(1)} %copy-done, s32[8,256]{1,0:T(8,128)S(1)} %reshape.10.lab_ref), custom_call_target="tpu_custom_call" | custom-call | tf_op jit(solution)/shard_map/affinities/pallas_call | solution.py:229
  47.1 1.0 %copy.8 = f32[2048,128]{1,0:T(8,128)} copy(f32[2048,128]{1,0:T(8,128)S(1)} %get-tuple-element.8) | data formatting | bytes 2097152
  48.1 0.5 %copy.9 = f32[128]{0:T(128)} copy(f32[128]{0:T(128)S(1)} %bitcast.1) | data formatting | bytes 1024
Async XLA Ops:
  2.0 1.2 %copy-start = (bf16[2048,256]{1,0:T(8,128)(2,1)S(1)}, bf16[2048,256]{1,0:T(8,128)(2,1)}, u32[]{:S(2)}) copy-start(bf16[2048,256]{1,0:T(8,128)(2,1)} %emb_ref.1) | copy-start | bytes 3145732

commit v3 on v2

--- a/solution.py
+++ b/solution.py
@@ -190,8 +190,7 @@
     parts[me, 0:1, :] = mass
 
     def send_part(o, _):
-        remote(parts.at[me], parts.at[me], part_send.at[o], part_recv.at[o],
-               lax.rem(me + o, n)).start()
+        remote(parts.at[me], parts.at[me], part_send, part_recv, lax.rem(me + o, n)).start()
         return 0
 
     lax.fori_loop(1, n, send_part, 0)
@@ -209,13 +208,10 @@
 
     lax.fori_loop(0, chunks, end_sends, 0)
 
-    def end_part(o, _):
-        source = lax.rem(me - o + n, n)
-        remote(parts.at[me], parts.at[source], part_send.at[o], part_recv.at[o],
-               lax.rem(me + o, n)).wait()
-        return 0
-
-    lax.fori_loop(1, n, end_part, 0)
+    all_parts = remote(parts.at[pl.ds(0, n - 1)], parts.at[pl.ds(0, n - 1)],
+                       part_send, part_recv, other)
+    all_parts.wait_send()
+    all_parts.wait_recv()
 
     masses = jnp.sum(parts[:, 0:1, :], axis=0)
     counts = jnp.sum(parts[:, 1:2, :], axis=0)
@@ -241,7 +237,7 @@
             pltpu.VMEM((CLUSTERS, rows), jnp.float32),
             pltpu.VMEM((n, 8, CLUSTERS), jnp.float32),
             dma, dma((3, rows // META)), dma((3, rows // META)), dma, dma, dma((4,)), dma((4,)),
-            dma((n,)), dma((n,)),
+            dma, dma,
         ],
         compiler_params=pltpu.CompilerParams(
             collective_id=0, has_side_effects=True, vmem_limit_bytes=48 * 2**20),

time: 48.8 us -> 48.5 us (level)
  no operation moved by 1% of the time
where the time goes in v3:
time: 48.5 us; the launch traced here: 48.3 us
  Pallas kernels  43.6 us (90%)
  local copies, waits for them, and re-layouts  3.41 us (7%)
  between operations  1.29 us (3%)
    pallas_call x1, Pallas kernels, local(): pl.pallas_call(functools.partial(kernel, n, factor), out_shape=(jax.Shape...  43.6 us
    unnamed x4, local copies, waits for them, and re-layouts  2.71 us

profile of v3, /device:TPU:0, one launch (start us, length us, event | category | flops | bytes accessed | tf_op | source)
XLA Modules:
  0.0 48.3 jit_solution(15685189900442234496)
XLA Ops:
  1.3 0.7 %reshape.10.lab_ref = s32[8,256]{1,0:T(8,128)S(1)} reshape(s32[2048]{0:T(1024)} %param.4) | data formatting | bytes 16384 | tf_op jit(solution)/shard_map/reshape | solution.py:245
  2.0 0.0 copy-start
  2.0 1.2 %copy-done = bf16[2048,256]{1,0:T(8,128)(2,1)S(1)} copy-done((bf16[2048,256]{1,0:T(8,128)(2,1)S(1)}, bf16[2048,256]{1,0:T(8,128)(2,1)}, u32[]{:S(2)}) %copy-start) | copy-done | bytes 1048600
  3.2 43.6 %affinities.1 = (f32[2048,128]{1,0:T(8,128)S(1)}, f32[1,128]{1,0:T(1,128)S(1)}) custom-call(f32[1]{0:T(128)S(6)} %copy.7.rate_ref, bf16[2048,256]{1,0:T(8,128)(2,1)S(1)} %copy-done, s32[8,256]{1,0:T(8,128)S(1)} %reshape.10.lab_ref), custom_call_target="tpu_custom_call" | custom-call | tf_op jit(solution)/shard_map/affinities/pallas_call | solution.py:225
  46.8 1.0 %copy.8 = f32[2048,128]{1,0:T(8,128)} copy(f32[2048,128]{1,0:T(8,128)S(1)} %get-tuple-element.8) | data formatting | bytes 2097152
  47.8 0.5 %copy.9 = f32[128]{0:T(128)} copy(f32[128]{0:T(128)S(1)} %bitcast.1) | data formatting | bytes 1024
Async XLA Ops:
  2.0 1.2 %copy-start = (bf16[2048,256]{1,0:T(8,128)(2,1)S(1)}, bf16[2048,256]{1,0:T(8,128)(2,1)}, u32[]{:S(2)}) copy-start(bf16[2048,256]{1,0:T(8,128)(2,1)} %emb_ref.1) | copy-start | bytes 3145732

commit v4 on v3

--- a/solution.py
+++ b/solution.py
@@ -86,8 +86,8 @@
     to_meta = [remote(lab_ref, meta.at[2 - o], meta_send.at[i], meta_recv.at[i],
                       lax.rem(me + o + n, n)) for i, o in enumerate(NEXT_TO)]
 
+    to_other.start()
     to_near(0).start()
-    to_other.start()
     for copy in to_meta:
         copy.start()
 
@@ -227,7 +227,7 @@
         out_shape=(jax.ShapeDtypeStruct((rows, CLUSTERS), jnp.float32),
                    jax.ShapeDtypeStruct((1, CLUSTERS), jnp.float32)),
         in_specs=[pl.BlockSpec(memory_space=pltpu.SMEM),
-                  pl.BlockSpec(memory_space=pl.ANY),
+                  pl.BlockSpec(memory_space=pltpu.HBM),
                   pl.BlockSpec(memory_space=pltpu.VMEM)],
         out_specs=[pl.BlockSpec(memory_space=pltpu.VMEM)] * 2,
         scratch_shapes=[

time: 48.5 us -> 48.5 us (level)
  no operation moved by 1% of the time
where the time goes in v4:
time: 48.5 us; the launch traced here: 48.3 us
  Pallas kernels  43.6 us (90%)
  local copies, waits for them, and re-layouts  3.41 us (7%)
  between operations  1.29 us (3%)
    pallas_call x1, Pallas kernels, local(): pl.pallas_call(functools.partial(kernel, n, factor), out_shape=(jax.Shape...  43.6 us
    unnamed x4, local copies, waits for them, and re-layouts  2.71 us

profile of v4, /device:TPU:0, one launch (start us, length us, event | category | flops | bytes accessed | tf_op | source)
XLA Modules:
  0.0 48.3 jit_solution(5248280438995793272)
XLA Ops:
  1.3 0.7 %reshape.10.lab_ref = s32[8,256]{1,0:T(8,128)S(1)} reshape(s32[2048]{0:T(1024)} %param.4) | data formatting | bytes 16384 | tf_op jit(solution)/shard_map/reshape | solution.py:245
  2.0 0.0 copy-start
  2.0 1.2 %copy-done = bf16[2048,256]{1,0:T(8,128)(2,1)S(1)} copy-done((bf16[2048,256]{1,0:T(8,128)(2,1)S(1)}, bf16[2048,256]{1,0:T(8,128)(2,1)}, u32[]{:S(2)}) %copy-start) | copy-done | bytes 1048600
  3.2 43.6 %affinities.1 = (f32[2048,128]{1,0:T(8,128)S(1)}, f32[1,128]{1,0:T(1,128)S(1)}) custom-call(f32[1]{0:T(128)S(6)} %copy.7.rate_ref, bf16[2048,256]{1,0:T(8,128)(2,1)S(1)} %copy-done, s32[8,256]{1,0:T(8,128)S(1)} %reshape.10.lab_ref), custom_call_target="tpu_custom_call" | custom-call | tf_op jit(solution)/shard_map/affinities/pallas_call | solution.py:225
  46.8 1.0 %copy.8 = f32[2048,128]{1,0:T(8,128)} copy(f32[2048,128]{1,0:T(8,128)S(1)} %get-tuple-element.8) | data formatting | bytes 2097152
  47.8 0.5 %copy.9 = f32[128]{0:T(128)} copy(f32[128]{0:T(128)S(1)} %bitcast.1) | data formatting | bytes 1024
Async XLA Ops:
  2.0 1.2 %copy-start = (bf16[2048,256]{1,0:T(8,128)(2,1)S(1)}, bf16[2048,256]{1,0:T(8,128)(2,1)}, u32[]{:S(2)}) copy-start(bf16[2048,256]{1,0:T(8,128)(2,1)} %emb_ref.1) | copy-start | bytes 3145732
